TPU v7x, 32 devices: a whole 2x2x4 slice. The times are simulated.
32 devices in a mesh: fsdp: 16 (over z, y, x), dp: 2 (over core).
Axes of the slice: x: 2, y: 2, z: 4, core: 2. Of those that a mesh axis runs over, the one named last changes fastest.
Arguments:
- tokens: bfloat16 [65536, 512], P(('fsdp', 'dp')), may hold values from -6 to 6
- cotangent: bfloat16 [65536, 512], P(('fsdp', 'dp')), may hold values from -6 to 6
- segment_ids: int32 [64, 1024], P(('fsdp', 'dp')), may hold values from 0 to 5, as said below
- valid_counts: int32 [64], P(('fsdp', 'dp')), may hold values from 768 to 960, as said below
- weight_qkv: float32 [512, 1536], P('fsdp'), may hold values from -0.25 to 0.25
- weight_out: float32 [512, 512], P('fsdp'), may hold values from -1 to 1
- weight_up: float32 [512, 2048], P('fsdp'), may hold values from -0.25 to 0.25
- weight_down: float32 [2048, 512], P('fsdp'), may hold values from -0.125 to 0.125
- vectors: float32 [8, 512], P(None, 'fsdp'), may hold values from -1.2 to 2.6, as said below
- up_bias: float32 [2048], P('fsdp'), may hold values from -1.5 to 1.5
- momentum_qkv: float32 [512, 1536], P('fsdp'), may hold values from -8 to 8
- momentum_out: float32 [512, 512], P('fsdp'), may hold values from -8 to 8
- momentum_up: float32 [512, 2048], P('fsdp'), may hold values from -8 to 8
- momentum_down: float32 [2048, 512], P('fsdp'), may hold values from -8 to 8
- momentum_vectors: float32 [8, 512], P(None, 'fsdp'), may hold values from -32 to 32
- momentum_bias: float32 [2048], P('fsdp'), may hold values from -4 to 4
- squares_qkv: float32 [512, 1536], P('fsdp'), may hold values from 1.6384 to 6.5536
- squares_out: float32 [512, 512], P('fsdp'), may hold values from 1.6384 to 6.5536
- squares_up: float32 [512, 2048], P('fsdp'), may hold values from 1.6384 to 6.5536
- squares_down: float32 [2048, 512], P('fsdp'), may hold values from 1.6384 to 6.5536
- squares_vectors: float32 [8, 512], P(None, 'fsdp'), may hold values from 26.2144 to 104.8576
- squares_bias: float32 [2048], P('fsdp'), may hold values from 0.524288 to 2.097152
Outputs:
- layer_out: bfloat16 [65536, 512], P(('fsdp', 'dp'))
- token_grad: float32 [65536, 512], P(('fsdp', 'dp'))
- grad_norm: float32 [], replicated
- weight_qkv_new: float32 [512, 1536], P('fsdp')
- weight_out_new: float32 [512, 512], P('fsdp')
- weight_up_new: float32 [512, 2048], P('fsdp')
- weight_down_new: float32 [2048, 512], P('fsdp')
- vectors_new: float32 [8, 512], P(None, 'fsdp')
- up_bias_new: float32 [2048], P('fsdp')
- momentum_qkv_new: float32 [512, 1536], P('fsdp')
- momentum_out_new: float32 [512, 512], P('fsdp')
- momentum_up_new: float32 [512, 2048], P('fsdp')
- momentum_down_new: float32 [2048, 512], P('fsdp')
- momentum_vectors_new: float32 [8, 512], P(None, 'fsdp')
- momentum_bias_new: float32 [2048], P('fsdp')
- squares_qkv_new: float32 [512, 1536], P('fsdp')
- squares_out_new: float32 [512, 512], P('fsdp')
- squares_up_new: float32 [512, 2048], P('fsdp')
- squares_down_new: float32 [2048, 512], P('fsdp')
- squares_vectors_new: float32 [8, 512], P(None, 'fsdp')
- squares_bias_new: float32 [2048], P('fsdp')
Inputs may be any that keep to these rules, and one draw needn't show every extreme that they name: `segment_ids`: within a packed sequence the ids number its images 0, 1, 2 and on in order, each image 192 or 384 positions long; positions from the sequence's valid count on hold 5. `valid_counts`: the total length of the images of the sequence, a multiple of 192. `vectors`: rows 0 and 5 are positive.
All inputs are finite; a program needn't handle non-finite values.
Results may differ from a plain program's by a relative error of at most 0.017.
The roundings to bfloat16 on the way count: a program that leaves them out, or rounds other values in their place, can miss the bound.
Values may be sent and summed in bfloat16 or wider, within the bound.
A program may use at most 256 MiB of HBM per device.

v0:
```python
import functools
import math

import jax
import jax.numpy as jnp
from jax import lax
from jax.experimental import pallas as pl
from jax.experimental.pallas import tpu as pltpu
from jax.sharding import PartitionSpec as P

D = 512
HEADS = 8
HEAD_DIM = 64
FF = 2048
SEQ = 1024
IMG = 192
BLOCKS = 5
STEP = 5
PARAMS = 3151872
GROUP = 256
PER_GROUP = GROUP // HEAD_DIM

F32 = jnp.float32
BF16 = jnp.bfloat16

norm_eps = 1e-06
adam_eps = 1e-08
decay_rate = 0.05
beta_first = 0.5
beta_second = 0.5
masked_score = -1e30


def dot(left, right):
    return lax.dot_general(left, right, (((1,), (0,)), ((), ())), preferred_element_type=F32)


def dot_nt(left, right):
    return lax.dot_general(left, right, (((1,), (1,)), ((), ())), preferred_element_type=F32)


def dot_tn(left, right):
    return lax.dot_general(left, right, (((0,), (0,)), ((), ())), preferred_element_type=F32)


def norm_forward(values, gain, shift):
    center = values - jnp.mean(values, axis=-1, keepdims=True)
    spread = lax.rsqrt(jnp.mean(center * center, axis=-1, keepdims=True) + norm_eps)
    hat = center * spread
    return hat * gain + shift, hat, spread


def norm_backward(incoming, hat, spread, gain):
    scaled = incoming * gain
    return spread * (
        scaled
        - jnp.mean(scaled, axis=-1, keepdims=True)
        - hat * jnp.mean(scaled * hat, axis=-1, keepdims=True)
    )


def gelu_pair(values):
    half = 0.5 * (1.0 + lax.erf(values * (1.0 / math.sqrt(2.0))))
    bell = jnp.exp(-0.5 * values * values) * (1.0 / math.sqrt(2.0 * math.pi))
    return values * half, half + values * bell


def col_sum(values):
    return jnp.sum(values, axis=0, keepdims=True)


def head_of_lane():
    return lax.broadcasted_iota(jnp.int32, (1, GROUP), 1) // HEAD_DIM


def stack_heads(rows):
    head = head_of_lane()
    zero = jnp.zeros_like(rows)
    return jnp.concatenate([jnp.where(head == h, rows, zero) for h in range(PER_GROUP)], axis=0)


def unstack_heads(stacked):
    head = head_of_lane()
    n = stacked.shape[0] // PER_GROUP
    rows = stacked[(PER_GROUP - 1) * n :]
    for h in range(PER_GROUP - 2, -1, -1):
        rows = jnp.where(head == h, stacked[h * n : (h + 1) * n], rows)
    return rows


def links(seg, counts, s):
    return [
        (seg[s, b * IMG] == seg[s, (b + 1) * IMG]) & ((b + 1) * IMG < counts[s])
        for b in range(BLOCKS - 1)
    ]


def neighbour(b, linked):
    below = slice((b + 1) * IMG, (b + 2) * IMG) if b < BLOCKS - 1 else None
    above = slice((b - 1) * IMG, b * IMG) if b > 0 else None
    with_below = linked[b] if b < BLOCKS - 1 else jnp.bool_(False)
    with_above = linked[b - 1] if b > 0 else jnp.bool_(False)
    offset = jnp.where(with_below | with_above, 0.0, masked_score)
    return below, above, with_below, with_above, offset


def other_rows(ref, cols, below, above, with_below):
    if above is None:
        return ref[below, cols]
    if below is None:
        return ref[above, cols]
    return jnp.where(with_below, ref[below, cols], ref[above, cols])


def attend_block(query, keys, values, offset):
    stacked = stack_heads(query * jnp.asarray(HEAD_DIM**-0.5, BF16))
    scores = dot_nt(keys, stacked)
    own, other = scores[:IMG], scores[IMG:]
    top = jnp.maximum(
        jnp.max(own, axis=0, keepdims=True), jnp.max(other, axis=0, keepdims=True) + offset
    )
    own = jnp.exp(own - top)
    other = jnp.exp(other - (top - offset))
    total = col_sum(own) + col_sum(other)
    inverse = 1.0 / total
    probs = jnp.concatenate([own * inverse, other * inverse], axis=0).astype(BF16)
    return unstack_heads(dot_tn(probs, values)), top + jnp.log(total)


def attend_block_backward(query, keys, values, grad, lse, offset):
    stacked = stack_heads(query * jnp.asarray(HEAD_DIM**-0.5, BF16))
    grads = stack_heads(grad)
    scores = dot_nt(keys, stacked)
    grad_probs = dot_nt(values, grads)
    own = jnp.exp(scores[:IMG] - lse)
    other = jnp.exp(scores[IMG:] - (lse - offset))
    own_t = own * grad_probs[:IMG]
    other_t = other * grad_probs[IMG:]
    delta = col_sum(own_t) + col_sum(other_t)
    grad_scores = jnp.concatenate([own_t - own * delta, other_t - other * delta], axis=0)
    grad_scores = grad_scores.astype(BF16)
    probs = jnp.concatenate([own, other], axis=0).astype(BF16)
    grad_values = dot(probs, grads)
    grad_keys = dot(grad_scores, stacked)
    grad_query = unstack_heads(dot_tn(grad_scores, keys)) * (HEAD_DIM**-0.5)
    return grad_query, grad_keys, grad_values


def forward_kernel(chunk, seg, counts, tokens, vectors, low_qkv, qkv, attended, lse):
    s = pl.program_id(0)
    bias = jnp.concatenate([vectors[2:3, :], jnp.zeros((1, D), F32), vectors[3:4, :]], axis=1)
    for c in range(SEQ // chunk):
        rows = slice(c * chunk, (c + 1) * chunk)
        normed, _, _ = norm_forward(tokens[rows, :].astype(F32), vectors[0:1, :], vectors[1:2, :])
        qkv[rows, :] = (dot(normed.astype(BF16), low_qkv[...]) + bias).astype(BF16)
    linked = links(seg, counts, s)
    for g in range(D // GROUP):
        query_cols, key_cols, value_cols = [
            slice(j * D + g * GROUP, j * D + (g + 1) * GROUP) for j in range(3)
        ]
        out_cols = slice(g * GROUP, (g + 1) * GROUP)
        for b in range(BLOCKS):
            rows = slice(b * IMG, (b + 1) * IMG)
            below, above, with_below, with_above, offset = neighbour(b, linked)
            keys = jnp.concatenate(
                [qkv[rows, key_cols], other_rows(qkv, key_cols, below, above, with_below)], axis=0
            )
            own_values = qkv[rows, value_cols]
            values = jnp.concatenate(
                [own_values, other_rows(qkv, value_cols, below, above, with_below)], axis=0
            )
            mixed, block_lse = attend_block(qkv[rows, query_cols], keys, values, offset)
            mixed = mixed.astype(BF16)
            if b == BLOCKS - 1:
                mixed = jnp.where(b * IMG >= counts[s], own_values, mixed)
            attended[rows, out_cols] = mixed
            lse[g * BLOCKS + b] = block_lse
        attended[BLOCKS * IMG :, out_cols] = qkv[BLOCKS * IMG :, value_cols]


def feed_kernel(
    rows_in,
    chunk,
    counts,
    tokens,
    cotangent,
    attended,
    vectors,
    up_bias,
    low_out,
    low_up,
    low_down,
    layer_out,
    grad_resid,
    grad_attended,
    grad_down,
    grad_up,
    grad_out_w,
    grad_vectors,
    grad_bias,
):
    i = pl.program_id(0)

    @pl.when(i == 0)
    def _():
        for ref in (grad_down, grad_up, grad_out_w, grad_vectors, grad_bias):
            ref[...] = jnp.zeros_like(ref)

    per = SEQ // rows_in
    mixed = attended[...]
    resid = tokens[...].astype(F32) + (dot(mixed, low_out[...]) + vectors[4:5, :])
    normed, hat, spread = norm_forward(resid, vectors[5:6, :], vectors[6:7, :])
    low_two = normed.astype(BF16)
    position = (i % per) * rows_in + lax.broadcasted_iota(jnp.int32, (rows_in, 1), 0)
    grad = jnp.where(position < counts[i // per], cotangent[...].astype(F32), 0.0)
    grad_low = grad.astype(BF16)
    out = jnp.zeros((rows_in, D), F32)
    grad_two = jnp.zeros((rows_in, D), F32)
    for c in range(FF // chunk):
        cols = slice(c * chunk, (c + 1) * chunk)
        hidden = dot(low_two, low_up[:, cols]) + up_bias[:, cols]
        grad_active = dot_nt(grad_low, low_down[cols, :])
        active, slope = gelu_pair(hidden)
        active = active.astype(BF16)
        grad_hidden = grad_active * slope
        grad_hidden_low = grad_hidden.astype(BF16)
        out += dot(active, low_down[cols, :])
        grad_bias[:, cols] += col_sum(grad_hidden)
        grad_down[cols, :] += dot_tn(active, grad_low)
        grad_up[:, cols] += dot_tn(low_two, grad_hidden_low)
        grad_two += dot_nt(grad_hidden_low, low_up[:, cols])
    layer_out[...] = (resid + (out + vectors[7:8, :])).astype(BF16)
    back = grad + norm_backward(grad_two, hat, spread, vectors[5:6, :])
    back_low = back.astype(BF16)
    grad_resid[...] = back
    grad_out_w[...] += dot_tn(mixed, back_low)
    grad_attended[...] = dot_nt(back_low, low_out[...]).astype(BF16)
    grad_vectors[4:5, :] += col_sum(back)
    grad_vectors[5:6, :] += col_sum(grad_two * hat)
    grad_vectors[6:7, :] += col_sum(grad_two)
    grad_vectors[7:8, :] += col_sum(grad)


def backward_kernel(
    chunk,
    seg,
    counts,
    tokens,
    vectors,
    low_qkv,
    qkv,
    grad_attended,
    grad_resid,
    lse,
    token_grad,
    grad_qkv_w,
    grad_vectors,
    grad_qkv,
    key_sum,
    value_sum,
):
    s = pl.program_id(0)

    @pl.when(s == 0)
    def _():
        grad_qkv_w[...] = jnp.zeros_like(grad_qkv_w)
        grad_vectors[...] = jnp.zeros_like(grad_vectors)

    linked = links(seg, counts, s)
    padded = (BLOCKS - 1) * IMG >= counts[s]
    covered = slice(0, BLOCKS * IMG)
    tail = slice(BLOCKS * IMG, SEQ)
    for g in range(D // GROUP):
        query_cols, key_cols, value_cols = [
            slice(j * D + g * GROUP, j * D + (g + 1) * GROUP) for j in range(3)
        ]
        grad_cols = slice(g * GROUP, (g + 1) * GROUP)
        query_bias = jnp.zeros((1, GROUP), F32)
        for b in range(BLOCKS):
            rows = slice(b * IMG, (b + 1) * IMG)
            below, above, with_below, with_above, offset = neighbour(b, linked)
            keys = jnp.concatenate(
                [qkv[rows, key_cols], other_rows(qkv, key_cols, below, above, with_below)], axis=0
            )
            values = jnp.concatenate(
                [qkv[rows, value_cols], other_rows(qkv, value_cols, below, above, with_below)],
                axis=0,
            )
            grad = grad_attended[rows, grad_cols]
            grad_query, grad_keys, grad_values = attend_block_backward(
                qkv[rows, query_cols], keys, values, grad, lse[g * BLOCKS + b], offset
            )
            own_keys, own_values = grad_keys[:IMG], grad_values[:IMG]
            if b == BLOCKS - 1:
                grad_query = jnp.where(padded, 0.0, grad_query)
                own_keys = jnp.where(padded, 0.0, own_keys)
                own_values = jnp.where(padded, grad.astype(F32), own_values)
            query_bias += col_sum(grad_query)
            grad_qkv[rows, query_cols] = grad_query.astype(BF16)
            if b > 0:
                own_keys += jnp.where(with_above, key_sum[rows, :], 0.0)
                own_values += jnp.where(with_above, value_sum[rows, :], 0.0)
            key_sum[rows, :] = own_keys
            value_sum[rows, :] = own_values
            if below is not None:
                key_sum[below, :] = grad_keys[IMG:]
                value_sum[below, :] = grad_values[IMG:]
            if above is not None:
                key_sum[above, :] += jnp.where(with_above, grad_keys[IMG:], 0.0)
                value_sum[above, :] += jnp.where(with_above, grad_values[IMG:], 0.0)
        grad_tail = grad_attended[tail, grad_cols]
        grad_qkv[tail, query_cols] = jnp.zeros_like(grad_tail)
        grad_qkv[tail, key_cols] = jnp.zeros_like(grad_tail)
        grad_qkv[tail, value_cols] = grad_tail
        grad_qkv[covered, key_cols] = key_sum[...].astype(BF16)
        all_values = value_sum[...]
        grad_qkv[covered, value_cols] = all_values.astype(BF16)
        grad_vectors[2:3, grad_cols] += query_bias
        grad_vectors[3:4, grad_cols] += col_sum(all_values) + col_sum(grad_tail.astype(F32))
    for c in range(SEQ // chunk):
        rows = slice(c * chunk, (c + 1) * chunk)
        normed, hat, spread = norm_forward(
            tokens[rows, :].astype(F32), vectors[0:1, :], vectors[1:2, :]
        )
        grad = grad_qkv[rows, :]
        grad_qkv_w[...] += dot_tn(normed.astype(BF16), grad)
        grad_one = dot_nt(grad, low_qkv[...])
        token_grad[rows, :] = grad_resid[rows, :] + norm_backward(
            grad_one, hat, spread, vectors[0:1, :]
        )
        grad_vectors[0:1, :] += col_sum(grad_one * hat)
        grad_vectors[1:2, :] += col_sum(grad_one)


def vmem_params():
    return pltpu.CompilerParams(vmem_limit_bytes=60 * 2**20)


def by_rows(rows, cols):
    return pl.BlockSpec((rows, cols), lambda i: (i, 0))


def whole(*shape):
    return pl.BlockSpec(shape, lambda i: (0,) * len(shape))


def stats_spec():
    return pl.BlockSpec((2 * BLOCKS, 1, PER_GROUP * IMG), lambda i: (i, 0, 0))


def shaped(shape, dtype):
    return jax.ShapeDtypeStruct(shape, dtype)


SCALAR = pl.BlockSpec(memory_space=pltpu.SMEM)


def run_forward(seg, counts, tokens, vectors, low_qkv):
    rows = tokens.shape[0]
    seqs = rows // SEQ
    return pl.pallas_call(
        functools.partial(forward_kernel, 256),
        grid=(seqs,),
        in_specs=[SCALAR, SCALAR, by_rows(SEQ, D), whole(8, D), whole(D, 3 * D)],
        out_specs=[by_rows(SEQ, 3 * D), by_rows(SEQ, D), stats_spec()],
        out_shape=[
            shaped((rows, 3 * D), BF16),
            shaped((rows, D), BF16),
            shaped((seqs * 2 * BLOCKS, 1, PER_GROUP * IMG), F32),
        ],
        compiler_params=vmem_params(),
        name="attend_forward",
    )(seg, counts, tokens, vectors, low_qkv)


def run_feed(counts, tokens, cotangent, attended, vectors, up_bias, low_out, low_up, low_down):
    rows = tokens.shape[0]
    step = 512
    return pl.pallas_call(
        functools.partial(feed_kernel, step, 512),
        grid=(rows // step,),
        in_specs=[
            SCALAR,
            by_rows(step, D),
            by_rows(step, D),
            by_rows(step, D),
            whole(8, D),
            whole(1, FF),
            whole(D, D),
            whole(D, FF),
            whole(FF, D),
        ],
        out_specs=[
            by_rows(step, D),
            by_rows(step, D),
            by_rows(step, D),
            whole(FF, D),
            whole(D, FF),
            whole(D, D),
            whole(8, D),
            whole(1, FF),
        ],
        out_shape=[
            shaped((rows, D), BF16),
            shaped((rows, D), F32),
            shaped((rows, D), BF16),
            shaped((FF, D), F32),
            shaped((D, FF), F32),
            shaped((D, D), F32),
            shaped((8, D), F32),
            shaped((1, FF), F32),
        ],
        compiler_params=vmem_params(),
        name="feed_forward",
    )(counts, tokens, cotangent, attended, vectors, up_bias, low_out, low_up, low_down)


def run_backward(seg, counts, tokens, vectors, low_qkv, qkv, grad_attended, grad_resid, lse):
    rows = tokens.shape[0]
    return pl.pallas_call(
        functools.partial(backward_kernel, 512),
        grid=(rows // SEQ,),
        in_specs=[
            SCALAR,
            SCALAR,
            by_rows(SEQ, D),
            whole(8, D),
            whole(D, 3 * D),
            by_rows(SEQ, 3 * D),
            by_rows(SEQ, D),
            by_rows(SEQ, D),
            stats_spec(),
        ],
        out_specs=[by_rows(SEQ, D), whole(D, 3 * D), whole(8, D)],
        out_shape=[
            shaped((rows, D), F32),
            shaped((D, 3 * D), F32),
            shaped((8, D), F32),
        ],
        scratch_shapes=[
            pltpu.VMEM((SEQ, 3 * D), BF16),
            pltpu.VMEM((BLOCKS * IMG, GROUP), F32),
            pltpu.VMEM((BLOCKS * IMG, GROUP), F32),
        ],
        compiler_params=vmem_params(),
        name="attend_backward",
    )(seg, counts, tokens, vectors, low_qkv, qkv, grad_attended, grad_resid, lse)


def adam_step(weight, moment, square, grad, factor, rate):
    clipped = grad * factor
    moment_new = beta_first * moment + (1.0 - beta_first) * clipped
    square_new = beta_second * square + (1.0 - beta_second) * clipped * clipped
    first_hat = moment_new / (1.0 - beta_first**STEP)
    second_hat = square_new / (1.0 - beta_second**STEP)
    weight_new = weight - rate * (
        first_hat / (jnp.sqrt(second_hat) + adam_eps) + decay_rate * weight
    )
    return (weight_new, moment_new, square_new)


RATES = (
    2.0 / math.sqrt(D),
    8.0 / math.sqrt(D),
    2.0 / math.sqrt(D),
    2.0 / math.sqrt(FF),
    0.5,
    0.5,
)


MESH = pl.DeviceIdType.MESH
COLS = 4


class Place:
    def __init__(self, planes):
        self.planes = planes
        self.i = lax.axis_index("fsdp")
        self.c = c = lax.axis_index("dp")
        self.q = q = lax.rem(self.i, COLS)
        self.z = self.i // COLS
        x, y = lax.rem(q, 2), q // 2
        self.qx = y * 2 + (1 - x)
        self.qy = (1 - y) * 2 + x
        self.qa = c * self.qx + (1 - c) * self.qy
        self.qb = c * self.qy + (1 - c) * self.qx
        self.qd = COLS - 1 - q
        self.at_a = (self.z * COLS + self.qa, c)
        self.at_b = (self.z * COLS + self.qb, c)
        self.at_x = (self.z * COLS + self.qx, c)
        self.at_y = (self.z * COLS + self.qy, c)
        self.at_d = (self.z * COLS + self.qd, c)
        self.partner = (self.i, 1 - c)

    def plane(self, step):
        return lax.rem(self.z + step, self.planes)

    def along(self, step):
        return (self.plane(step) * COLS + self.q, self.c)

    def greet(self):
        barrier = pltpu.get_barrier_semaphore()
        friends = [self.along(step) for step in range(1, self.planes)]
        friends += [self.at_a, self.at_b, self.at_d, self.partner]
        for device in friends:
            pl.semaphore_signal(barrier, inc=1, device_id=device, device_id_type=MESH)
        pl.semaphore_wait(barrier, len(friends))


def remote(source, target, send, recv, device):
    return pltpu.make_async_remote_copy(
        src_ref=source,
        dst_ref=target,
        send_sem=send,
        recv_sem=recv,
        device_id=device,
        device_id_type=MESH,
    )


class Gather:
    def __init__(self, place, full, send, recv):
        p, c = place, place.c
        n = p.planes
        self.pieces = n

        def move(k, plane, col, device):
            ref = full.at[plane, col, c]
            return remote(ref, ref, send.at[k], recv.at[k], device)

        self.to_z = [move(k, p.z, p.q, p.along(k + 1)) for k in range(n - 1)]
        base = n - 1
        self.to_a = [move(base + d, p.plane(n - d), p.q, p.at_a) for d in range(n)]
        self.to_b = [move(base + n + d, p.plane(n - d), p.q, p.at_b) for d in range(n)]
        self.on_b = [move(base + 2 * n + d, p.plane(n - d), p.qa, p.at_b) for d in range(n)]
        base += 3 * n
        self.to_core = [
            move(base + k, slice(None), col, p.partner)
            for k, col in enumerate((p.q, p.qa, p.qb, p.qd))
        ]

    @staticmethod
    def count(planes):
        return 4 * planes + 3

    def begin(self):
        for copy in self.to_z:
            copy.start()

    def begin_own(self):
        self.to_a[0].start()
        self.to_b[0].start()

    def spread(self):
        for k, copy in enumerate(self.to_z):
            copy.wait_recv()
            self.to_a[k + 1].start()
            self.to_b[k + 1].start()
        self.to_core[0].start()

    def forward(self):
        for k in range(self.pieces):
            self.to_a[k].wait_recv()
            self.on_b[k].start()
        self.to_core[1].start()

    def last(self):
        for copy in self.to_b:
            copy.wait_recv()
        self.to_core[2].start()
        for copy in self.on_b:
            copy.wait_recv()
        self.to_core[3].start()

    def arrive(self):
        for copy in self.to_core:
            copy.wait_recv()

    def drain(self):
        for copy in (*self.to_z, *self.to_a, *self.to_b, *self.on_b, *self.to_core):
            copy.wait_send()


class Scatter:
    def __init__(self, place, total, bufs, result, send, recv, squares):
        self.place, self.total, self.result, self.squares = place, total, result, squares
        self.in_c, self.out_b, self.in_b = bufs[:3]
        self.out_a, self.in_a, self.out_z, self.in_z = bufs[3:7]
        self.out_c = bufs[7]
        p = place
        self.order = (p.qa, p.qd, p.qb, p.q)
        self.to_core = [
            remote(self.out_c.at[k], self.in_c.at[k], send.at[k], recv.at[k], p.partner)
            for k in range(4)
        ]
        self.to_b = [
            remote(self.out_b.at[k], self.in_b.at[k], send.at[4 + k], recv.at[4 + k], p.at_b)
            for k in range(2)
        ]
        self.to_a = remote(self.out_a, self.in_a, send.at[6], recv.at[6], p.at_a)
        self.to_z = [
            remote(self.out_z.at[k], self.in_z.at[k], send.at[7 + k], recv.at[7 + k], p.along(k + 1))
            for k in range(p.planes - 1)
        ]
        n = 6 + p.planes
        half = result.at[p.c]
        self.to_both = remote(half, half, send.at[n], recv.at[n], p.partner)

    @staticmethod
    def count(planes):
        return planes + 7

    @staticmethod
    def buffers(planes, rows, cols, own=True):
        shapes = [(4, planes)] + [(2, planes)] * 2 + [(planes,)] * 2 + [(planes - 1,)] * 2
        shapes += [(4, planes)] if own else []
        return [pltpu.VMEM((*shape, rows, cols), BF16) for shape in shapes]

    def begin(self):
        for k in range(4):
            self.out_c[k] = self.total[:, self.order[k], 1 - self.place.c].astype(BF16)
            self.to_core[k].start()

    def second(self):
        p = self.place
        for k, col in ((1, p.qd), (0, p.qb)):
            self.to_core[k].wait_recv()
            mine = self.total[:, col, p.c] + self.in_c[k].astype(F32)
            self.out_b[k] = mine.astype(BF16)
            self.to_b[k].start()

    def first(self):
        p = self.place
        self.to_core[2].wait_recv()
        self.to_b[1].wait_recv()
        mine = self.total[:, p.qa, p.c] + self.in_c[2].astype(F32) + self.in_b[1].astype(F32)
        self.out_a[...] = mine.astype(BF16)
        self.to_a.start()

    def planes(self):
        p = self.place
        self.to_core[3].wait_recv()
        self.to_b[0].wait_recv()
        self.to_a.wait_recv()

        def mine(z):
            local = self.total[z, p.q, p.c] + self.in_c[3, z].astype(F32)
            return local + self.in_b[0, z].astype(F32) + self.in_a[z].astype(F32)

        for k in range(p.planes - 1):
            self.out_z[k] = mine(p.plane(k + 1)).astype(BF16)
            self.to_z[k].start()
        self.result[p.c] = mine(p.z)

    def finish(self):
        p = self.place
        for copy in self.to_z:
            copy.wait_recv()
        shard = self.result[p.c]
        for k in range(p.planes - 1):
            shard = shard + self.in_z[k].astype(F32)
        self.result[p.c] = shard
        self.to_both.start()
        square = shard * shard
        lanes = sum(square[:, k : k + 128] for k in range(0, square.shape[1], 128))
        self.squares[...] += jnp.sum(lanes.reshape(-1, 8, 128), axis=0)

    def drain(self):
        self.to_both.wait_recv()
        for copy in (*self.to_core, *self.to_b, self.to_a, *self.to_z, self.to_both):
            copy.wait_send()


def sum_over_all(place, part, out, slots, send, recv):
    p = place
    count = p.planes + COLS - 1
    out[0] = part
    copies = [remote(out.at[0], slots.at[count + 1], send.at[0], recv.at[0], p.partner)]
    copies[0].start()
    copies[0].wait_recv()
    chip = part + slots[count + 1]
    out[1] = chip
    slots[p.z] = chip
    lines = [
        remote(out.at[1], slots.at[p.z], send.at[k + 1], recv.at[k + 1], p.along(k + 1))
        for k in range(p.planes - 1)
    ]
    for copy in lines:
        copy.start()
    for copy in lines:
        copy.wait_recv()
    column = slots[0]
    for k in range(1, p.planes):
        column = column + slots[k]
    out[2] = column
    slots[p.planes + p.q] = column
    columns = [
        remote(out.at[2], slots.at[p.planes + p.q], send.at[n], recv.at[n], device)
        for n, device in enumerate((p.at_x, p.at_y, p.at_d), p.planes)
    ]
    for copy in columns:
        copy.start()
    for copy in columns:
        copy.wait_recv()
    total = slots[p.planes]
    for k in range(1, COLS):
        total = total + slots[p.planes + k]
    for copy in (*copies, *lines, *columns):
        copy.wait_send()
    return total


def small_shard(place, vectors, up_bias):
    def tile(rows):
        for axis, full in ((1, 128), (0, 8)):
            short = list(rows.shape)
            short[axis] = full - short[axis]
            if short[axis]:
                rows = jnp.concatenate([rows, jnp.zeros(short, F32)], axis=axis)
        return rows

    rows, bias = tile(vectors[...]), tile(up_bias[...])
    half = jnp.where(place.c == 0, rows, bias)
    return jnp.concatenate([half, jnp.zeros((8, 128), F32)], axis=0).astype(BF16)


ROWS = 512
SPAN = SEQ // IMG * IMG


def five(planes, rows, cols):
    return (planes, COLS, 2, rows, cols)


def flat(value):
    return value.reshape(-1, value.shape[-1])


def layer_kernel(planes, per, long, *refs):
    seg, counts, tokens, cotangent = refs[:4]
    shards, vector_shard, bias_shard = refs[4:8], refs[8], refs[9]
    layer_out, token_grad = refs[10:12]
    results, first_rows, norm, kept = refs[12:18], refs[18], refs[19], refs[20]
    full, small, vectors, up_bias = refs[21:25], refs[25], refs[26], refs[27]
    totals = refs[28:34]
    tok, cot, qkv, mixed, resid, lse, key_sum, value_sum = refs[34:42]
    grad_vectors, grad_bias = refs[42:44]
    bufs = refs[44:89]
    g_send, g_recv, s_send, s_recv = refs[89:93]
    out_tiles, in_tiles, t_send, t_recv, load_sem, out_sem, grad_sem = refs[93:100]
    square_sum = refs[100]
    full_qkv, full_out, full_up, full_down = full
    sum_out, sum_up, sum_down, sum_low, sum_high, sum_small = totals
    p = Place(planes)
    rows_local = tok.shape[0]
    seqs = rows_local // SEQ

    low_one = cot
    load_tokens = pltpu.make_async_copy(tokens, tok, load_sem.at[0])
    load_cotangent = pltpu.make_async_copy(cotangent, cot, load_sem.at[1])
    keep_low = pltpu.make_async_copy(low_one, kept, load_sem.at[2])
    recall_low = pltpu.make_async_copy(kept, low_one, load_sem.at[3])
    load_tokens.start()

    small[p.z, p.q, p.c] = small_shard(p, vector_shard, bias_shard)
    for shard, target in zip(shards, full):
        target[p.z, p.q, p.c] = shard[p.c].astype(BF16)
    p.greet()
    g_small, g_qkv, g_out, g_up, g_down = gathers = [
        Gather(p, ref, g_send.at[k], g_recv.at[k]) for k, ref in enumerate((small, *full))
    ]
    spare = [ref.at[:, :, 0] for ref in full[1:]]
    bufs = [[*bufs[7 * k : 7 * k + 7], spare[k]] for k in range(3)] + [
        bufs[21 + 8 * k : 29 + 8 * k] for k in range(3)
    ]
    scatters = [
        Scatter(p, total, bufs[k], results[k], s_send.at[k], s_recv.at[k], square_sum)
        for k, total in enumerate(totals)
    ]
    s_out, s_up, s_down, s_low, s_high, s_small = scatters
    g_small.begin()
    g_qkv.begin()
    for item in gathers:
        item.begin_own()
    g_small.spread()
    g_qkv.spread()
    for item in (g_out, g_up, g_down):
        item.begin()
    g_small.forward()
    g_qkv.forward()
    g_out.spread()
    g_small.last()
    g_qkv.last()
    g_small.arrive()
    for s in range(planes * COLS):
        rows = small[s // COLS, s % COLS, 0].astype(F32)
        bias = small[s // COLS, s % COLS, 1].astype(F32)
        vectors[:, s * per : (s + 1) * per] = rows[:8, :per]
        up_bias[:, s * long : (s + 1) * long] = bias[:1, :long]
    load_tokens.wait()
    g_qkv.arrive()

    qkv_bias = jnp.concatenate([vectors[2:3, :], jnp.zeros((1, D), F32), vectors[3:4, :]], axis=1)
    chunk = 256
    beside_qkv = {
        0: [g_out.forward],
        2: [g_up.spread],
        5: [g_out.last],
        7: [g_up.forward],
    }

    def stages_at(k, table):
        for at, stages in table.items():

            @pl.when(k == at)
            def _(stages=stages):
                for stage in stages:
                    stage()

    @pl.loop(0, rows_local // chunk)
    def _(k):
        rows = pl.ds(pl.multiple_of(k * chunk, chunk), chunk)
        normed, _, _ = norm_forward(tok[rows, :].astype(F32), vectors[0:1, :], vectors[1:2, :])
        low = normed.astype(BF16)
        low_one[rows, :] = low
        qkv[rows, :] = (dot(low, flat(full_qkv[...])) + qkv_bias).astype(BF16)
        stages_at(k, beside_qkv)

    g_down.spread()
    keep_low.start()

    def block_rows(s, b):
        return pl.ds(pl.multiple_of(s * SEQ + b * IMG, 64), IMG)

    def tail_rows(s):
        return pl.ds(pl.multiple_of(s * SEQ + SPAN, 64), SEQ - SPAN)

    def columns(g):
        return [slice(j * D + g * GROUP, j * D + (g + 1) * GROUP) for j in range(3)]

    def with_other(cols, s, b, with_below):
        own = qkv[block_rows(s, b), cols]
        if b == 0:
            other = qkv[block_rows(s, 1), cols]
        elif b == BLOCKS - 1:
            other = qkv[block_rows(s, b - 1), cols]
        else:
            other = jnp.where(
                with_below, qkv[block_rows(s, b + 1), cols], qkv[block_rows(s, b - 1), cols]
            )
        return jnp.concatenate([own, other], axis=0)

    for g in range(D // GROUP):
        query_cols, key_cols, value_cols = columns(g)
        own_cols = slice(g * GROUP, (g + 1) * GROUP)

        def attend(s):
            linked = links(seg, counts, s)
            for b in range(BLOCKS):
                _, _, with_below, _, offset = neighbour(b, linked)
                keys = with_other(key_cols, s, b, with_below)
                values = with_other(value_cols, s, b, with_below)
                block, block_lse = attend_block(
                    qkv[block_rows(s, b), query_cols], keys, values, offset
                )
                block = block.astype(BF16)
                if b == BLOCKS - 1:
                    block = jnp.where(b * IMG >= counts[s], values[:IMG], block)
                mixed[block_rows(s, b), own_cols] = block
                lse[(s * 2 + g) * BLOCKS + b] = block_lse
            mixed[tail_rows(s), own_cols] = qkv[tail_rows(s), value_cols]

        pl.loop(0, seqs)(attend)
        if g == 0:
            g_up.last()
            g_down.forward()
            keep_low.wait()
            load_cotangent.start()
        else:
            g_down.last()

    for item in (g_out, g_up, g_down):
        item.arrive()
    load_cotangent.wait()

    for ref in (sum_out, sum_up, sum_down, sum_small, grad_vectors, grad_bias, square_sum):
        ref[...] = jnp.zeros_like(ref)
    width = FF // planes

    def feed(i, carry):
        rows = pl.ds(pl.multiple_of(i * ROWS, ROWS), ROWS)
        block = mixed[rows, :]
        low_out = flat(full_out[...])
        res = tok[rows, :].astype(F32) + (dot(block, low_out) + vectors[4:5, :])
        normed, hat, spread = norm_forward(res, vectors[5:6, :], vectors[6:7, :])
        low_two = normed.astype(BF16)
        position = (i % (SEQ // ROWS)) * ROWS + lax.broadcasted_iota(jnp.int32, (ROWS, 1), 0)
        grad = jnp.where(position < counts[i // (SEQ // ROWS)], cot[rows, :].astype(F32), 0.0)
        grad_low = grad.astype(BF16)
        out = jnp.zeros((ROWS, D), F32)
        grad_two = jnp.zeros((ROWS, D), F32)
        for k in range(planes):
            cols = slice(k * width, (k + 1) * width)
            up = flat(full_up[:, :, :, :, cols])
            down = flat(full_down[k])
            hidden = dot(low_two, up) + up_bias[:, cols]
            grad_active = dot_nt(grad_low, down)
            active, slope = gelu_pair(hidden)
            active = active.astype(BF16)
            grad_hidden = grad_active * slope
            grad_hidden_low = grad_hidden.astype(BF16)
            out += dot(active, down)
            grad_bias[:, cols] += col_sum(grad_hidden)
            sum_down[k] += dot_tn(active, grad_low).reshape(sum_down.shape[1:])
            sum_up[:, :, :, :, cols] += dot_tn(low_two, grad_hidden_low).reshape(
                *sum_up.shape[:-1], width
            )
            grad_two += dot_nt(grad_hidden_low, up)
        cot[rows, :] = (res + (out + vectors[7:8, :])).astype(BF16)
        pltpu.make_async_copy(cot.at[rows], layer_out.at[rows], out_sem.at[i]).start()
        back = grad + norm_backward(grad_two, hat, spread, vectors[5:6, :])
        back_low = back.astype(BF16)
        resid[rows, :] = back
        sum_out[...] += dot_tn(block, back_low).reshape(sum_out.shape)
        mixed[rows, :] = dot_nt(back_low, low_out).astype(BF16)
        grad_vectors[4:5, :] += col_sum(back)
        grad_vectors[5:6, :] += col_sum(grad_two * hat)
        grad_vectors[6:7, :] += col_sum(grad_two)
        grad_vectors[7:8, :] += col_sum(grad)
        return carry

    lax.fori_loop(0, rows_local // ROWS, feed, 0)

    for item in gathers:
        item.drain()
    s_down.begin()
    s_up.begin()
    s_out.begin()
    parts = [slice(k * ROWS, (k + 1) * ROWS) for k in range(rows_local // ROWS)]
    layer_copies = [
        pltpu.make_async_copy(cot.at[rows], layer_out.at[rows], out_sem.at[k])
        for k, rows in enumerate(parts)
    ]

    def recall():
        for copy in layer_copies:
            copy.wait()
        recall_low.start()

    beside_attention = {
        (0, 0, 1): [s_down.second, s_up.second, s_out.second],
        (0, 1, 1): [s_down.first, recall],
        (1, 0, 1): [s_up.first, s_down.planes, s_low.second],
        (1, 1, 1): [s_out.first, s_up.planes],
    }
    for g in range(D // GROUP):
        query_cols, key_cols, value_cols = columns(g)
        own_cols = slice(g * GROUP, (g + 1) * GROUP)

        def attend_back(s, query_bias):
            linked = links(seg, counts, s)
            padded = (BLOCKS - 1) * IMG >= counts[s]
            for b in range(BLOCKS):
                below, above, with_below, with_above, offset = neighbour(b, linked)
                rows = slice(b * IMG, (b + 1) * IMG)
                keys = with_other(key_cols, s, b, with_below)
                values = with_other(value_cols, s, b, with_below)
                grad = mixed[block_rows(s, b), own_cols]
                grad_query, grad_keys, grad_values = attend_block_backward(
                    qkv[block_rows(s, b), query_cols],
                    keys,
                    values,
                    grad,
                    lse[(s * 2 + g) * BLOCKS + b],
                    offset,
                )
                own_keys, own_values = grad_keys[:IMG], grad_values[:IMG]
                if b == BLOCKS - 1:
                    grad_query = jnp.where(padded, 0.0, grad_query)
                    own_keys = jnp.where(padded, 0.0, own_keys)
                    own_values = jnp.where(padded, grad.astype(F32), own_values)
                query_bias += col_sum(grad_query)
                qkv[block_rows(s, b), query_cols] = grad_query.astype(BF16)
                if b > 0:
                    own_keys += jnp.where(with_above, key_sum[rows, :], 0.0)
                    own_values += jnp.where(with_above, value_sum[rows, :], 0.0)
                key_sum[rows, :] = own_keys
                value_sum[rows, :] = own_values
                if below is not None:
                    key_sum[below, :] = grad_keys[IMG:]
                    value_sum[below, :] = grad_values[IMG:]
                if above is not None:
                    key_sum[above, :] += jnp.where(with_above, grad_keys[IMG:], 0.0)
                    value_sum[above, :] += jnp.where(with_above, grad_values[IMG:], 0.0)
                stages_at(s, {k[1]: v for k, v in beside_attention.items() if k[::2] == (g, b)})
            covered = pl.ds(pl.multiple_of(s * SEQ, SEQ), SPAN)
            grad_tail = mixed[tail_rows(s), own_cols]
            qkv[tail_rows(s), query_cols] = jnp.zeros_like(grad_tail)
            qkv[tail_rows(s), key_cols] = jnp.zeros_like(grad_tail)
            qkv[tail_rows(s), value_cols] = grad_tail
            qkv[covered, key_cols] = key_sum[...].astype(BF16)
            all_values = value_sum[...]
            qkv[covered, value_cols] = all_values.astype(BF16)
            grad_vectors[3:4, own_cols] += col_sum(all_values) + col_sum(grad_tail.astype(F32))
            return query_bias

        grad_vectors[2:3, own_cols] = lax.fori_loop(
            0, seqs, attend_back, jnp.zeros((1, GROUP), F32)
        )
        if g == 0:
            recall_low.wait()
        total = (sum_low, sum_high)[g]
        for j, cols in enumerate(columns(g)):
            part = dot_tn(low_one[...], qkv[:, cols])
            total[:, :, :, :, j * GROUP : (j + 1) * GROUP] = part.reshape(*total.shape[:-1], GROUP)
        (s_low, s_high)[g].begin()
        if g == 1:
            s_low.first()
            s_out.planes()

    for s in range(planes * COLS):
        cols = slice(s * per, (s + 1) * per)
        sum_small[s // COLS, s % COLS, 0, 0:8, 0:per] = grad_vectors[:, cols]
        sum_small[s // COLS, s % COLS, 1, 0:1, 0:long] = grad_bias[:, s * long : (s + 1) * long]
    s_small.begin()

    beside_last = {
        0: [s_high.second, s_small.second, s_down.finish],
        1: [s_high.first, s_small.first, s_low.planes],
        2: [s_high.planes, s_small.planes, s_up.finish],
        3: [s_out.finish, s_low.finish],
    }

    @pl.loop(0, rows_local // ROWS)
    def _(k):
        rows = pl.ds(pl.multiple_of(k * ROWS, ROWS), ROWS)
        _, hat, spread = norm_forward(tok[rows, :].astype(F32), vectors[0:1, :], vectors[1:2, :])
        grad_one = dot_nt(qkv[rows, :], flat(full_qkv[...]))
        resid[rows, :] += norm_backward(grad_one, hat, spread, vectors[0:1, :])
        pltpu.make_async_copy(resid.at[rows], token_grad.at[rows], grad_sem.at[k]).start()
        grad_vectors[0:1, :] += col_sum(grad_one * hat)
        grad_vectors[1:2, :] += col_sum(grad_one)
        stages_at(k, beside_last)

    for item in (s_high, s_small):
        item.finish()
    part = square_sum[...]
    gain_sum, shift_sum = grad_vectors[0:1, :], grad_vectors[1:2, :]
    rows = [
        item[:, k * 128 : (k + 1) * 128] for item in (gain_sum, shift_sum) for k in range(D // 128)
    ]
    tiles = jnp.concatenate([*rows, part], axis=0)
    tiles = sum_over_all(p, tiles, out_tiles, in_tiles, t_send, t_recv)
    first_rows[...] = tiles[:8]
    norm[...] = tiles[8:]
    for item in scatters:
        item.drain()
    for k, rows in enumerate(parts):
        pltpu.make_async_copy(resid.at[rows], token_grad.at[rows], grad_sem.at[k]).wait()


def run_layer(planes, seg, counts, tokens, cotangent, masters):
    halves = [item.reshape(2, item.shape[0] // 2, item.shape[1]) for item in masters[:4]]
    per, long = masters[4].shape[1], masters[5].shape[0]
    rows = tokens.shape[0]
    seqs = rows // SEQ
    shapes = [item.shape[1:] for item in halves]
    group = (shapes[0][0], 3 * GROUP)
    sums = [*shapes[1:], group, group, (16, 128)]
    vmem = pl.BlockSpec(memory_space=pltpu.VMEM)
    hbm = pl.BlockSpec(memory_space=pl.ANY)
    dma = pltpu.SemaphoreType.DMA
    scratch = [pltpu.VMEM(five(planes, *shape), BF16) for shape in (*shapes, (16, 128))]
    scratch += [pltpu.VMEM((8, D), F32), pltpu.VMEM((1, FF), F32)]
    scratch += [pltpu.VMEM(five(planes, *shape), F32) for shape in sums]
    scratch += [
        pltpu.VMEM((rows, D), BF16),
        pltpu.VMEM((rows, D), BF16),
        pltpu.VMEM((rows, 3 * D), BF16),
        pltpu.VMEM((rows, D), BF16),
        pltpu.VMEM((rows, D), F32),
        pltpu.VMEM((seqs * 2 * BLOCKS, 1, PER_GROUP * IMG), F32),
        pltpu.VMEM((SPAN, GROUP), F32),
        pltpu.VMEM((SPAN, GROUP), F32),
        pltpu.VMEM((8, D), F32),
        pltpu.VMEM((1, FF), F32),
    ]
    for k, shape in enumerate(sums):
        scratch += Scatter.buffers(planes, *shape, own=k >= 3)
    scratch += [dma((5, Gather.count(planes)))] * 2 + [dma((6, Scatter.count(planes)))] * 2
    scratch += [pltpu.VMEM((3, 16, 128), F32), pltpu.VMEM((planes + COLS + 1, 16, 128), F32)]
    scratch += [dma((planes + 3,))] * 2 + [dma((4,))] + [dma((rows // ROWS,))] * 2
    scratch += [pltpu.VMEM((8, 128), F32)]
    return pl.pallas_call(
        functools.partial(layer_kernel, planes, per, long),
        in_specs=[SCALAR, SCALAR, hbm, hbm] + [vmem] * 6,
        out_specs=[hbm, hbm] + [vmem] * 8 + [hbm],
        out_shape=[shaped((rows, D), BF16), shaped((rows, D), F32)]
        + [shaped((2, *shape), F32) for shape in sums]
        + [shaped((8, 128), F32), shaped((8, 128), F32), shaped((rows, D), BF16)],
        scratch_shapes=scratch,
        compiler_params=pltpu.CompilerParams(
            vmem_limit_bytes=63 * 2**20, collective_id=1, has_side_effects=True
        ),
        name="layer",
    )(seg, counts, tokens, cotangent, *halves, masters[4], masters[5].reshape(1, -1))


def update_kernel(bound, pieces, *refs):
    sources, targets, rest = refs[:28], refs[28:49], refs[49:]
    held, middles = rest[:26], rest[26:28]
    fresh, total = rest[28:46], rest[46]
    in_sems, out_sems, mid_sems = rest[47:]
    into, out_of = [], []
    for n, (source, middle, target) in enumerate(zip(sources[26:], middles, targets[:2])):
        rows = source.shape[0] // pieces
        for k in range(pieces):
            part, sem = pl.ds(k * rows, rows), mid_sems.at[n, k]
            into.append(pltpu.make_async_copy(source.at[part], middle.at[part], sem))
            out_of.append(pltpu.make_async_copy(middle.at[part], target.at[part], sem))
    loads = [
        pltpu.make_async_copy(source, target, in_sems.at[k])
        for k, (source, target) in enumerate(zip(sources, held))
    ]
    stores = [
        pltpu.make_async_copy(source, target, out_sems.at[k])
        for k, (source, target) in enumerate(zip((total, *fresh), targets[2:]))
    ]
    for copy in (*loads, *into):
        copy.start()
    for copy in loads:
        copy.wait()
    results, first_rows, norm = held[:6], held[6], held[7]
    masters, moments, squares = held[8:14], held[14:20], held[20:26]
    i = lax.axis_index("fsdp")
    first = first_rows[...]
    every = jnp.sum(norm[...], axis=(0, 1), keepdims=True)
    every = every + jnp.sum(first * first, axis=(0, 1), keepdims=True)
    root = jnp.sqrt(every)
    total[...] = root
    stores[0].start()
    factor = jnp.minimum(1.0, bound / root)
    out, up, down, low, high, small = results
    low, high = flat(low[...]), flat(high[...])
    qkv = [item[:, j * GROUP : (j + 1) * GROUP] for j in range(3) for item in (low, high)]
    per = masters[4].shape[1]
    rows = small[0, 0:8, 0:per]
    line = lax.broadcasted_iota(jnp.int32, (8, 1), 0)
    for s in range(D // per):
        at = s * per
        gain = first[at // 128 : at // 128 + 1, at % 128 : at % 128 + per]
        at = D + at
        shift = first[at // 128 : at // 128 + 1, at % 128 : at % 128 + per]
        mine = jnp.where(line == 0, gain, jnp.where(line == 1, shift, rows))
        rows = jnp.where(i == s, mine, rows)
    grads = (
        jnp.concatenate(qkv, axis=1),
        flat(out[...]),
        flat(up[...]),
        flat(down[...]),
        rows,
        small[1, 0:1, 0 : masters[5].shape[1]],
    )
    for k in range(6):
        new = adam_step(
            masters[k][...], moments[k][...], squares[k][...], grads[k], factor, RATES[k]
        )
        for at, item in zip((k, 6 + k, 12 + k), new):
            fresh[at][...] = item
            stores[1 + at].start()
        for first_half, second_half in zip(into[k : k + 2], out_of[k : k + 2]) if k % 2 == 0 else ():
            first_half.wait()
            second_half.start()
    for first_half, second_half in zip(into[6:], out_of[6:]):
        first_half.wait()
        second_half.start()
    for copy in (*stores, *out_of):
        copy.wait()


def run_update(bound, layer_out, token_grad, results, masters, moments, squares):
    def lines(items):
        return [*items[:5], items[5].reshape(1, -1)]

    state = lines(masters) + lines(moments) + lines(squares)
    held = [*results, *state]
    hbm = pl.BlockSpec(memory_space=pl.ANY)
    dma = pltpu.SemaphoreType.DMA
    pieces = 4
    passed = (layer_out, token_grad)
    done = pl.pallas_call(
        functools.partial(update_kernel, bound, pieces),
        in_specs=[hbm] * 28,
        out_specs=[hbm] * 21,
        out_shape=[shaped(item.shape, item.dtype) for item in passed]
        + [shaped((1, 1), F32)]
        + [shaped(item.shape, F32) for item in state],
        scratch_shapes=[pltpu.VMEM(item.shape, item.dtype) for item in (*held, *passed, *state)]
        + [pltpu.VMEM((1, 1), F32), dma((26,)), dma((19,)), dma((2, pieces))],
        compiler_params=vmem_params(),
        name="update_state",
    )(*held, *passed)
    fresh = [item.reshape(-1) if k % 6 == 5 else item for k, item in enumerate(done[3:])]
    return (done[0], done[1], done[2].reshape(()), *fresh)


def compute(tokens, cotangent, segment_ids, valid_counts, full):
    low_qkv, low_out, low_up, low_down, vectors, up_bias = full
    qkv, attended, lse = run_forward(segment_ids, valid_counts, tokens, vectors, low_qkv)
    (
        layer_out,
        grad_resid,
        grad_attended,
        grad_down,
        grad_up,
        grad_out_w,
        late,
        grad_bias,
    ) = run_feed(
        valid_counts, tokens, cotangent, attended, vectors, up_bias, low_out, low_up, low_down
    )
    token_grad, grad_qkv_w, early = run_backward(
        segment_ids,
        valid_counts,
        tokens,
        vectors,
        low_qkv,
        qkv,
        grad_attended,
        grad_resid,
        lse,
    )
    return layer_out, token_grad, (grad_qkv_w, grad_out_w, grad_up, grad_down), early, late, grad_bias


def fast_body(tokens, cotangent, segment_ids, valid_counts, *state):
    masters, moments, squares = state[:6], state[6:12], state[12:18]
    wide = lax.axis_size("fsdp")
    layer_out, token_grad, *results, _ = run_layer(
        wide // COLS, segment_ids, valid_counts, tokens, cotangent, masters
    )
    bound = 0.005 * math.sqrt(tokens.shape[0] * wide * lax.axis_size("dp") * PARAMS)
    return run_update(bound, layer_out, token_grad, results, masters, moments, squares)


def plain_body(tokens, cotangent, segment_ids, valid_counts, *state):
    masters, moments, squares = state[:6], state[6:12], state[12:18]
    wide = lax.axis_size("fsdp")
    replicas = lax.axis_size("dp")
    low = [item.astype(BF16) for item in masters]
    full = [
        lax.all_gather(item, "fsdp", axis=1 if k == 4 else 0, tiled=True)
        for k, item in enumerate(low)
    ]
    full[4] = full[4].astype(F32)
    full[5] = full[5].astype(F32).reshape(1, FF)
    layer_out, token_grad, totals, early, late, bias = compute(
        tokens, cotangent, segment_ids, valid_counts, full
    )
    grads = []
    for k, item in enumerate((*totals, early + late, bias.reshape(FF))):
        shard = lax.psum_scatter(item, "fsdp", scatter_dimension=1 if k == 4 else 0, tiled=True)
        grads.append(lax.psum(shard.astype(BF16), "dp").astype(F32))
    local_total = jnp.sum(grads[0] * grads[0])
    for item in grads[1:]:
        local_total = local_total + jnp.sum(item * item)
    grad_norm = jnp.sqrt(lax.psum(local_total, "fsdp"))
    bound = 0.005 * math.sqrt(tokens.shape[0] * wide * replicas * PARAMS)
    factor = jnp.minimum(1.0, bound / grad_norm)
    fresh = [
        adam_step(masters[k], moments[k], squares[k], grads[k], factor, RATES[k]) for k in range(6)
    ]
    return (
        layer_out,
        token_grad,
        grad_norm,
        *(item[0] for item in fresh),
        *(item[1] for item in fresh),
        *(item[2] for item in fresh),
    )


def solution(mesh):
    rows = P(("fsdp", "dp"), None)
    state = (
        P("fsdp", None),
        P("fsdp", None),
        P("fsdp", None),
        P("fsdp", None),
        P(None, "fsdp"),
        P("fsdp"),
    )
    wide, replicas = mesh.shape["fsdp"], mesh.shape["dp"]
    fits = replicas == 2 and wide == COLS * COLS
    return jax.shard_map(
        fast_body if fits else plain_body,
        mesh=mesh,
        in_specs=(rows, rows, rows, P(("fsdp", "dp")), *state, *state, *state),
        out_specs=(rows, rows, P(), *state, *state, *state),
        check_vma=False,
    )
```

profile of v0, /device:TPU:0, one launch (start us, length us, event | category | flops | bytes accessed | tf_op | source)
XLA Modules:
  0.0 145.0 jit_solution(8629028221343108024)
XLA Ops:
  0.7 135.8 %layer.1 = (bf16[2048,512]{1,0:T(8,128)(2,1)}, f32[2048,512]{1,0:T(8,128)}, f32[2,16,512]{2,1,0:T(8,128)}, f32[2,16,2048]{2,1,0:T(8,128)}, f32[2,64,512]{2,1,0:T...) custom-call(s32[2,1024]{1,0:T(2,128)} %refs_0_.1, ...), custom_call_target="tpu_custom_call" | custom-call | tf_op jit(solution)/shard_map/layer/pallas_call | solution.py:1095
  136.5 8.3 %update_state.1 = (bf16[2048,512]{1,0:T(8,128)(2,1)}, f32[2048,512]{1,0:T(8,128)}, f32[1,1]{1,0:T(1,128)}, f32[32,1536]{1,0:T(8,128)}, f32[32,512]{1,0:T(8,128)}...) custom-call(f32[2,16,512]{2,1,0:T(8,128)} %get-tuple-element.52.refs, ...), custom_call_target="tpu_custom_call" | custom-call | tf_op jit(solution)/shard_map/update_state/pallas_call | solution.py:1192
where the time goes:
time: 145 us
  Pallas kernels  144 us (99%)
    pallas_call x1, Pallas kernels, run_layer(): pl.pallas_call(functools.partial(layer_kernel, planes, per, long), in_spe...  136 us
    pallas_call x1, Pallas kernels, run_update(): pl.pallas_call(functools.partial(update_kernel, bound, pieces), in_specs=...  8.34 us

commit v1 on v0

--- a/solution.py
+++ b/solution.py
@@ -1131,6 +1131,9 @@
         copy.start()
     for copy in loads:
         copy.wait()
+    for first_half, second_half in zip(into, out_of):
+        first_half.wait()
+        second_half.start()
     results, first_rows, norm = held[:6], held[6], held[7]
     masters, moments, squares = held[8:14], held[14:20], held[20:26]
     i = lax.axis_index("fsdp")
@@ -1169,12 +1172,6 @@
         for at, item in zip((k, 6 + k, 12 + k), new):
             fresh[at][...] = item
             stores[1 + at].start()
-        for first_half, second_half in zip(into[k : k + 2], out_of[k : k + 2]) if k % 2 == 0 else ():
-            first_half.wait()
-            second_half.start()
-    for first_half, second_half in zip(into[6:], out_of[6:]):
-        first_half.wait()
-        second_half.start()
     for copy in (*stores, *out_of):
         copy.wait()
 

time: 145 us -> 144 us (level)
  no operation moved by 1% of the time
where the time goes in v1:
time: 144 us
  Pallas kernels  143 us (99%)
    pallas_call x1, Pallas kernels, run_layer(): pl.pallas_call(functools.partial(layer_kernel, planes, per, long), in_spe...  136 us
    pallas_call x1, Pallas kernels, run_update(): pl.pallas_call(functools.partial(update_kernel, bound, pieces), in_specs=...  7.41 us

profile of v1, /device:TPU:0, one launch (start us, length us, event | category | flops | bytes accessed | tf_op | source)
XLA Modules:
  0.0 144.1 jit_solution(18360324763456932340)
XLA Ops:
  0.7 135.8 %layer.1 = (bf16[2048,512]{1,0:T(8,128)(2,1)}, f32[2048,512]{1,0:T(8,128)}, f32[2,16,512]{2,1,0:T(8,128)}, f32[2,16,2048]{2,1,0:T(8,128)}, f32[2,64,512]{2,1,0:T...) custom-call(s32[2,1024]{1,0:T(2,128)} %refs_0_.1, ...), custom_call_target="tpu_custom_call" | custom-call | tf_op jit(solution)/shard_map/layer/pallas_call | solution.py:1095
  136.5 7.4 %update_state.1 = (bf16[2048,512]{1,0:T(8,128)(2,1)}, f32[2048,512]{1,0:T(8,128)}, f32[1,1]{1,0:T(1,128)}, f32[32,1536]{1,0:T(8,128)}, f32[32,512]{1,0:T(8,128)}...) custom-call(f32[2,16,512]{2,1,0:T(8,128)} %get-tuple-element.52.refs, ...), custom_call_target="tpu_custom_call" | custom-call | tf_op jit(solution)/shard_map/update_state/pallas_call | solution.py:1189
